TPU v7x, 32 devices: a whole 2x2x4 slice. The times are simulated.
32 devices in a mesh: ctx: 8 (over y, x, core), head: 4 (over z).
Axes of the slice: x: 2, y: 2, z: 4, core: 2. Of those that a mesh axis runs over, the one named last changes fastest.
Arguments:
- tokens: bfloat16 [1024, 8192], P('ctx', 'head'), may hold values from -6 to 6
- norm_gain: float32 [8192], replicated, may hold values from 0.1 to 1.9
- query_weight: bfloat16 [8192, 8192], P(None, 'head'), may hold values from -0.0625 to 0.0625
- key_weight: bfloat16 [8192, 1024], P(None, 'head'), may hold values from -0.0625 to 0.0625
- value_weight: bfloat16 [8192, 1024], P(None, 'head'), may hold values from -0.0625 to 0.0625
- cache_keys: bfloat16 [8192, 1024], P('ctx', 'head'), may hold values from -200 to 200
- cache_values: bfloat16 [8192, 1024], P('ctx', 'head'), may hold values from -6 to 6
- cache_lengths: int32 [8], replicated, may hold values from 2 to 1024, as said below
- start_position: int32 [1], replicated, may hold values from 1 to 8192
Outputs:
- attended: bfloat16 [1024, 8192], P('ctx', 'head')
Inputs may be any that keep to these rules, and one draw needn't show every extreme that they name: `cache_lengths`: entry c counts the live rows of cache shard c from its first row; some shard is full.
All inputs are finite; a program needn't handle non-finite values.
Results may differ from a plain program's by a relative error of at most 0.015.
The roundings to bfloat16 on the way count: a program that leaves them out, or rounds other values in their place, can miss the bound.
Values may be sent and summed in bfloat16 or wider, within the bound.
A program may use at most 192 MiB of HBM per device.

v0:
```python
import functools

import jax
import jax.numpy as jnp
from jax import lax
from jax.experimental import pallas as pl
from jax.experimental.pallas import tpu as pltpu
from jax.sharding import PartitionSpec as P

HEAD_DIM = 128
MESH = pl.DeviceIdType.MESH

epsilon = 1e-05
rope_base = 500000.0
masked_score = -1e30
score_scale = HEAD_DIM ** (-0.5)
log2e = 1.4426950408889634


def project_kernel(
    n, heads, tok_hbm, gain_ref, wq_hbm, wk_hbm, wv_hbm, ck_hbm, cv_hbm, cos_ref, sin_ref,
    q_out, k_out, v_out, fk_out, fv_out,
    wq, wk, wv, toks, normed, fk, fv,
    w_sem, own_sem, tok_send, tok_recv, c_send, c_recv, f_send, f_recv,
):
    me = lax.axis_index("ctx")
    h = lax.axis_index("head")
    chips = n // 2
    chip = me // 2
    core = me % 2
    sibling = chip * 2 + 1 - core
    width = toks.shape[2]
    square_plane = chips == 4
    across, along = chip // 2, chip % 2
    near = (None, across * 2 + 1 - along, (1 - across) * 2 + along, 3 - chip)

    def to_peer(d):
        found = near[d] if square_plane else (chip + d) % chips
        return found * 2 + core

    def from_chip(d):
        return near[d] if square_plane else (chip + chips - d) % chips

    weights = [
        pltpu.make_async_copy(src, dst, w_sem.at[i])
        for i, (src, dst) in enumerate(((wk_hbm, wk), (wv_hbm, wv), (wq_hbm, wq)))
    ]

    barrier = pltpu.get_barrier_semaphore()
    for d in range(1, chips):
        pl.semaphore_signal(
            barrier, inc=1, device_id=(to_peer(d), h), device_id_type=MESH
        )
    pl.semaphore_signal(barrier, inc=1, device_id=(sibling, h), device_id_type=MESH)
    for step in (1, heads - 1):
        pl.semaphore_signal(
            barrier, inc=1, device_id=(me, (h + step) % heads), device_id_type=MESH
        )
    pl.semaphore_wait(barrier, chips + 2)

    def token_copy(way, s):
        origin = h - (s - 1) if way == 0 else h + (s - 1)
        target = h + 1 if way == 0 else h - 1
        src = tok_hbm if s == 1 else toks.at[origin]
        return pltpu.make_async_remote_copy(
            src_ref=src,
            dst_ref=toks.at[origin],
            send_sem=tok_send.at[way, s - 1],
            recv_sem=tok_recv.at[way, s - 1],
            device_id=(me, target),
            device_id_type=MESH,
        )

    def sends(way, s):
        if way == 0:
            return (h >= s - 1) & (h + 1 < heads)
        return (h + s - 1 < heads) & (h >= 1)

    def receives(way, s):
        return h >= s if way == 0 else h + s < heads

    def received(way, s):
        origin = h - s if way == 0 else h + s
        return pltpu.make_async_remote_copy(
            src_ref=toks.at[origin],
            dst_ref=toks.at[origin],
            send_sem=tok_send.at[way, s - 1],
            recv_sem=tok_recv.at[way, s - 1],
            device_id=(me, (h + 1) % heads),
            device_id_type=MESH,
        )

    def block_copy(array, src, out, origin, target, sends_, recvs_, d):
        return pltpu.make_async_remote_copy(
            src_ref=src,
            dst_ref=out.at[origin],
            send_sem=sends_.at[array, d],
            recv_sem=recvs_.at[array, d],
            device_id=(target, h),
            device_id_type=MESH,
        )

    def spread(array, src, out, direct):
        copies = []
        for d in range(1, direct):
            copies.append(block_copy(array, src, out, me, to_peer(d), c_send, c_recv, d))
        copies.append(block_copy(array, src, out, me, sibling, c_send, c_recv, 0))
        for copy in copies:
            copy.start()
        own = pltpu.make_async_copy(src, out.at[me], own_sem.at[array])
        own.start()
        return copies, own

    for way in (0, 1):
        @pl.when(sends(way, 1))
        def _():
            token_copy(way, 1).start()
    own_tok = pltpu.make_async_copy(tok_hbm, toks.at[h], own_sem.at[4])
    own_tok.start()
    direct = 3 if square_plane else chips
    pending = [spread(0, ck_hbm, k_out, direct), spread(1, cv_hbm, v_out, direct)]
    outs = (k_out, v_out, fk_out, fv_out)
    forwards = []

    def arrived(array, d):
        origin = from_chip(d) * 2 + core
        out = outs[array]
        block_copy(array, out.at[origin], out, origin, sibling, c_send, c_recv, d).wait_recv()
        return out.at[origin], out, origin

    def forward(array, d):
        src, out, origin = arrived(array, d)
        hand_on(array, src, out, origin, d)

    def hand_on(array, src, out, origin, d):
        copy = block_copy(array, src, out, origin, sibling, f_send, f_recv, d)
        copy.start()
        forwards.append(copy)

    def relay(array, source, target):
        src, out, origin = arrived(array, source)
        copy = block_copy(array, src, out, origin, to_peer(target), c_send, c_recv, 3)
        copy.start()
        forwards.append(copy)
        hand_on(array, src, out, origin, source)

    for copy in weights:
        copy.start()

    for s in range(1, heads):
        for way in (0, 1):
            @pl.when(receives(way, s))
            def _():
                received(way, s).wait_recv()
            if s + 1 < heads:
                @pl.when(sends(way, s + 1))
                def _():
                    token_copy(way, s + 1).start()
        if square_plane and s == max(1, heads - 2):
            relay(0, 1, 2)
            relay(1, 2, 1)
    if square_plane:
        forward(0, 2)
        forward(1, 1)
    own_tok.wait()

    square = jnp.zeros((toks.shape[1], 1), jnp.float32)
    for o in range(heads):
        part = toks[o].astype(jnp.float32)
        square += jnp.sum(part * part, -1, keepdims=True)
    inverse = lax.rsqrt(square / (heads * width) + epsilon)
    for o in range(heads):
        cols = slice(o * width, (o + 1) * width)
        part = toks[o].astype(jnp.float32)
        normed[:, cols] = (part * inverse * gain_ref[:, cols]).astype(jnp.bfloat16)

    def rotated(u):
        return (u * cos_ref[...] + pltpu.roll(u, HEAD_DIM // 2, 1) * sin_ref[...]).astype(
            jnp.bfloat16
        )

    weights[0].wait()
    keys = jnp.dot(normed[...], wk[...], preferred_element_type=jnp.float32)
    for j in range(wk.shape[1] // HEAD_DIM):
        cols = slice(j * HEAD_DIM, (j + 1) * HEAD_DIM)
        fk[:, cols] = rotated(keys[:, cols])
    weights[1].wait()
    fv[...] = jnp.dot(normed[...], wv[...], preferred_element_type=jnp.float32).astype(
        jnp.bfloat16
    )
    pending += [spread(2, fk, fk_out, chips), spread(3, fv, fv_out, chips)]
    weights[2].wait()
    tile = 2 * HEAD_DIM

    @pl.loop(0, wq.shape[1] // tile)
    def _(t):
        cols = pl.ds(pl.multiple_of(t * tile, tile), tile)
        found = jnp.dot(normed[...], wq[:, cols], preferred_element_type=jnp.float32)
        for j in range(2):
            q_out[2 * t + j] = rotated(found[:, j * HEAD_DIM : (j + 1) * HEAD_DIM])

    for d in (3,) if square_plane else range(1, chips):
        forward(0, d)
        forward(1, d)
    for d in range(1, chips):
        forward(2, d)
        forward(3, d)
    for array, out in enumerate(outs):
        block_copy(array, out.at[sibling], out, sibling, sibling, c_send, c_recv, 0).wait_recv()
        for d in range(1, chips):
            origin = from_chip(d) * 2 + 1 - core
            block_copy(array, out.at[origin], out, origin, sibling, f_send, f_recv, d).wait_recv()
    for copy in forwards:
        copy.wait_send()
    for copies, own in pending:
        own.wait()
        for copy in copies:
            copy.wait_send()
    for s in range(1, heads):
        for way in (0, 1):
            @pl.when(sends(way, s))
            def _():
                token_copy(way, s).wait_send()


def attend_kernel(n, scalars, q_ref, k_ref, v_ref, fk_ref, fv_ref, out_ref, num, den, top):
    c = pl.program_id(1)
    group, tok_rows = q_ref.shape[0], q_ref.shape[1]
    cache_rows = k_ref.shape[1]
    fresh_rows = fk_ref.shape[0]

    def weigh(q, keys, values, bias):
        scores = lax.dot_general(
            q, keys, (((1,), (1,)), ((), ())), preferred_element_type=jnp.float32
        )
        scores = scores + bias
        high = jnp.max(scores, -1, keepdims=True)
        weights = jnp.exp2((scores - high) * (score_scale * log2e))
        total = jnp.sum(weights, -1, keepdims=True)
        mixed = jnp.dot(
            weights.astype(jnp.bfloat16), values, preferred_element_type=jnp.float32
        )
        return mixed, high * score_scale, total

    @pl.when(c == 0)
    def _():
        num[...] = jnp.zeros_like(num)
        den[...] = jnp.zeros_like(den)
        top[...] = jnp.full_like(top, masked_score)

    length = scalars[jnp.minimum(c, n - 1)]
    pieces = 4
    pair = 2 if group % 2 == 0 else 1

    def cache_step(live):
        bias = jnp.where(
            lax.broadcasted_iota(jnp.int32, (1, live), 1) < length, 0.0, masked_score
        ).astype(jnp.float32)
        for i in range(group // pair):
            rows = slice(i * pair * tok_rows, (i + 1) * pair * tok_rows)
            q = q_ref[i * pair : (i + 1) * pair].reshape(pair * tok_rows, HEAD_DIM)
            mixed, high, total = weigh(q, k_ref[0, :live], v_ref[0, :live], bias)
            part = (mixed / total).astype(jnp.bfloat16).astype(jnp.float32)
            lse = high + jnp.log(total)
            before = top[rows]
            now = jnp.maximum(before, lse)
            keep = jnp.exp(before - now)
            add = jnp.exp(lse - now)
            num[rows] = num[rows] * keep + part * add
            den[rows] = den[rows] * keep + add
            top[rows] = now

    def fresh_step(live):
        first = scalars[n] * tok_rows
        seen = lax.broadcasted_iota(jnp.int32, (tok_rows, live), 1) <= (
            first + lax.broadcasted_iota(jnp.int32, (tok_rows, live), 0)
        )
        bias = jnp.where(seen, 0.0, masked_score).astype(jnp.float32)
        for i in range(group):
            rows = slice(i * tok_rows, (i + 1) * tok_rows)
            mixed, high, total = weigh(q_ref[i], fk_ref[:live], fv_ref[:live], bias)
            before = top[rows]
            now = jnp.maximum(before, high)
            keep = jnp.exp(before - now)
            add = jnp.exp(high - now)
            value = (num[rows] * keep + mixed * add) / (den[rows] * keep + total * add)
            out_ref[:, i * HEAD_DIM : (i + 1) * HEAD_DIM] = value.astype(jnp.bfloat16)

    step = cache_rows // pieces
    fresh_step_rows = fresh_rows // pieces
    fresh_length = (scalars[n] + 1) * tok_rows
    for piece in range(pieces):
        @pl.when((c < n) & (length > piece * step) & (length <= (piece + 1) * step))
        def _():
            cache_step((piece + 1) * step)

        @pl.when(
            (c == n)
            & (fresh_length > piece * fresh_step_rows)
            & (fresh_length <= (piece + 1) * fresh_step_rows)
        )
        def _():
            fresh_step((piece + 1) * fresh_step_rows)


def body(
    tokens, norm_gain, query_weight, key_weight, value_weight, cache_keys, cache_values,
    cache_lengths, start_position,
):
    n = lax.axis_size("ctx")
    heads = lax.axis_size("head")
    rank = lax.axis_index("ctx")
    tok_rows, width = tokens.shape
    model = query_weight.shape[0]
    kv_cols = key_weight.shape[1]
    q_cols = query_weight.shape[1]
    cache_rows = cache_keys.shape[0]
    local_kv = kv_cols // HEAD_DIM
    local_q = q_cols // HEAD_DIM
    group = local_q // local_kv
    half = HEAD_DIM // 2
    position = (start_position[0] + rank * tok_rows + jnp.arange(tok_rows, dtype=jnp.int32)).astype(
        jnp.float32
    )
    freqs = jnp.power(
        jnp.float32(rope_base), -2.0 * jnp.arange(half, dtype=jnp.float32) / HEAD_DIM
    )
    angles = position[:, None] * freqs[None, :]
    cosine, sine = jnp.cos(angles), jnp.sin(angles)
    cos_table = jnp.concatenate([cosine, cosine], -1)
    sin_table = jnp.concatenate([-sine, sine], -1)

    anywhere = pl.BlockSpec(memory_space=pl.ANY)
    vmem = pl.BlockSpec(memory_space=pltpu.VMEM)
    bf16 = jnp.bfloat16
    chips = n // 2
    q, all_k, all_v, fresh_k, fresh_v = pl.pallas_call(
        functools.partial(project_kernel, n, heads),
        out_shape=[
            jax.ShapeDtypeStruct((local_q, tok_rows, HEAD_DIM), bf16),
            jax.ShapeDtypeStruct((n, cache_rows, kv_cols), bf16),
            jax.ShapeDtypeStruct((n, cache_rows, kv_cols), bf16),
            jax.ShapeDtypeStruct((n, tok_rows, kv_cols), bf16),
            jax.ShapeDtypeStruct((n, tok_rows, kv_cols), bf16),
        ],
        in_specs=[anywhere, vmem, anywhere, anywhere, anywhere, anywhere, anywhere, vmem, vmem],
        out_specs=[vmem, anywhere, anywhere, anywhere, anywhere],
        scratch_shapes=[
            pltpu.VMEM((model, q_cols), bf16),
            pltpu.VMEM((model, kv_cols), bf16),
            pltpu.VMEM((model, kv_cols), bf16),
            pltpu.VMEM((heads, tok_rows, width), bf16),
            pltpu.VMEM((tok_rows, model), bf16),
            pltpu.VMEM((tok_rows, kv_cols), bf16),
            pltpu.VMEM((tok_rows, kv_cols), bf16),
            pltpu.SemaphoreType.DMA((3,)),
            pltpu.SemaphoreType.DMA((5,)),
            pltpu.SemaphoreType.DMA((2, heads)),
            pltpu.SemaphoreType.DMA((2, heads)),
            pltpu.SemaphoreType.DMA((4, chips)),
            pltpu.SemaphoreType.DMA((4, chips)),
            pltpu.SemaphoreType.DMA((4, chips)),
            pltpu.SemaphoreType.DMA((4, chips)),
        ],
        compiler_params=pltpu.CompilerParams(
            collective_id=0, has_side_effects=True, vmem_limit_bytes=56 * 2**20
        ),
        name="gather_project",
    )(
        tokens, norm_gain[None, :], query_weight, key_weight, value_weight, cache_keys,
        cache_values, cos_table, sin_table,
    )

    fresh_k = fresh_k.reshape(n * tok_rows, kv_cols)
    fresh_v = fresh_v.reshape(n * tok_rows, kv_cols)
    scalars = jnp.concatenate([cache_lengths, rank.astype(jnp.int32)[None]])
    cache_spec = pl.BlockSpec(
        (1, cache_rows, HEAD_DIM), lambda g, c, s: (jnp.minimum(c, n - 1), 0, g)
    )
    fresh_spec = pl.BlockSpec((n * tok_rows, HEAD_DIM), lambda g, c, s: (0, g))
    rows = group * tok_rows
    return pl.pallas_call(
        functools.partial(attend_kernel, n),
        out_shape=jax.ShapeDtypeStruct((tok_rows, q_cols), bf16),
        grid_spec=pltpu.PrefetchScalarGridSpec(
            num_scalar_prefetch=1,
            grid=(local_kv, n + 1),
            in_specs=[
                pl.BlockSpec((group, tok_rows, HEAD_DIM), lambda g, c, s: (g, 0, 0)),
                cache_spec,
                cache_spec,
                fresh_spec,
                fresh_spec,
            ],
            out_specs=pl.BlockSpec((tok_rows, group * HEAD_DIM), lambda g, c, s: (0, g)),
            scratch_shapes=[
                pltpu.VMEM((rows, HEAD_DIM), jnp.float32),
                pltpu.VMEM((rows, 1), jnp.float32),
                pltpu.VMEM((rows, 1), jnp.float32),
            ],
        ),
        compiler_params=pltpu.CompilerParams(vmem_limit_bytes=48 * 2**20),
        name="attend",
    )(scalars, q, all_k, all_v, fresh_k, fresh_v)


def solution(mesh):
    in_specs = (
        P("ctx", "head"),
        P(),
        P(None, "head"),
        P(None, "head"),
        P(None, "head"),
        P("ctx", "head"),
        P("ctx", "head"),
        P(),
        P(),
    )
    out_specs = P("ctx", "head")
    return jax.shard_map(body, mesh=mesh, in_specs=in_specs, out_specs=out_specs, check_vma=False)
```

profile of v0, /device:TPU:7, one launch (start us, length us, event | category | flops | bytes accessed | tf_op | source)
XLA Modules:
  0.0 108.9 jit_solution(7240920527975810638)
XLA Ops:
  0.7 0.7 pad_add_fusion.scalars
  1.4 0.3 fusion
  1.7 0.8 pad_maximum_fusion
  2.5 57.3 %gather_project.1 = (bf16[16,128,128]{2,1,0:T(8,128)(2,1)}, bf16[8,1024,256]{2,1,0:T(8,128)(2,1)}, bf16[8,1024,256]{2,1,0:T(8,128)(2,1)}, bf16[8,128,256]{2,1,0:T(8,128)(2,1)}, bf16[8,128,256]{2,1,0:T(8,128)(2,1)}) custom-call(bf16[128,2048]{1,0:T(8,128)(2,1)} %tok_hbm.1, f32[1,8192]{1,0:T(1,128)} %bitcast.8, bf16[8192,2048]{1,0:T(8,128)(2,1)} %wq_hbm.1, ...), custom_call_target="tpu_custom_call" | custom-call | tf_op jit(solution)/shard_map/gather_project/pallas_call | solution.py:337
  59.8 0.0 copy-start
  59.8 2.2 %copy-done = bf16[8,1024,256]{2,1,0:T(8,128)(2,1)S(1)} copy-done((bf16[8,1024,256]{2,1,0:T(8,128)(2,1)S(1)}, bf16[8,1024,256]{2,1,0:T(8,128)(2,1)}, u32[]{:S(2)}) %copy-start) | copy-done | bytes 4194328
  62.0 0.0 copy-start.1
  62.0 1.0 copy-done.1
  63.0 0.0 copy-start.2
  63.1 1.0 copy-done.2
  64.1 0.0 copy-start.3
  64.1 1.0 copy-done.3
  65.1 43.8 %attend.1 = bf16[128,2048]{1,0:T(8,128)(2,1)} custom-call(s32[9]{0:T(128)S(1)} %pad_add_fusion.scalars, bf16[16,128,128]{2,1,0:T(8,128)(2,1)S(1)} %copy-done.1, bf16[8,1024,256]{2,1,0:T(8,128)(2,1)S(1)} %copy-done, bf16[8,1024,256]{2,1,0:T(8,128)(2,1)} %get-tuple-element.12.v_ref, bf16[1024,256]{1,0:T(8,128)(2,1)S(1)} %bitcast.6, bf16[1024,256]{1,0:T(8,128)(2,1)S(1)} %bitcast.7), custom_call_target="tpu_custom_call" | custom-call | tf_op jit(solution)/shard_map/attend/pallas_call | solution.py:382
  (2 shorter events, 0.0 us)
Async XLA Ops:
  59.8 2.2 %copy-start = (bf16[8,1024,256]{2,1,0:T(8,128)(2,1)S(1)}, bf16[8,1024,256]{2,1,0:T(8,128)(2,1)}, u32[]{:S(2)}) copy-start(bf16[8,1024,256]{2,1,0:T(8,128)(2,1)} %get-tuple-element.11.k_ref) | copy-start | bytes 12582916
  62.0 1.0 copy-start.1
  63.0 1.0 copy-start.2
  64.1 1.0 copy-start.3
where the time goes:
time: 108 us; the launch traced here: 109 us
  Pallas kernels  101 us (94%)
  local copies, waits for them, and re-layouts  5.3 us (5%)
  other arithmetic  1.82 us (2%)
    pallas_call x1, Pallas kernels, body(): pl.pallas_call(functools.partial(project_kernel, n, heads), out_shape=[ja...  57.3 us
    pallas_call x1, Pallas kernels, body(): pl.pallas_call(functools.partial(attend_kernel, n), out_shape=jax.ShapeDt...  43.8 us
    unnamed x8, local copies, waits for them, and re-layouts  5.3 us

commit v1 on v0

--- a/solution.py
+++ b/solution.py
@@ -231,14 +231,19 @@
 
     def weigh(q, keys, values, bias):
         scores = lax.dot_general(
-            q, keys, (((1,), (1,)), ((), ())), preferred_element_type=jnp.float32
-        )
-        scores = scores + bias
-        high = jnp.max(scores, -1, keepdims=True)
+            keys, q, (((1,), (1,)), ((), ())), preferred_element_type=jnp.float32
+        )
+        clear = scores.shape[0] - bias.shape[0]
+        if clear:
+            scores = jnp.concatenate([scores[:clear], scores[clear:] + bias], 0)
+        else:
+            scores = scores + bias
+        high = jnp.max(scores, 0, keepdims=True)
         weights = jnp.exp2((scores - high) * (score_scale * log2e))
-        total = jnp.sum(weights, -1, keepdims=True)
-        mixed = jnp.dot(
-            weights.astype(jnp.bfloat16), values, preferred_element_type=jnp.float32
+        total = jnp.sum(weights, 0, keepdims=True)
+        mixed = lax.dot_general(
+            values, weights.astype(jnp.bfloat16), (((0,), (0,)), ((), ())),
+            preferred_element_type=jnp.float32,
         )
         return mixed, high * score_scale, total
 
@@ -250,11 +255,13 @@
 
     length = scalars[jnp.minimum(c, n - 1)]
     pieces = 4
-    pair = 2 if group % 2 == 0 else 1
+    pair = group
 
     def cache_step(live):
         bias = jnp.where(
-            lax.broadcasted_iota(jnp.int32, (1, live), 1) < length, 0.0, masked_score
+            lax.broadcasted_iota(jnp.int32, (step, pair * tok_rows), 0) < length - (live - step),
+            0.0,
+            masked_score,
         ).astype(jnp.float32)
         for i in range(group // pair):
             rows = slice(i * pair * tok_rows, (i + 1) * pair * tok_rows)
@@ -262,29 +269,29 @@
             mixed, high, total = weigh(q, k_ref[0, :live], v_ref[0, :live], bias)
             part = (mixed / total).astype(jnp.bfloat16).astype(jnp.float32)
             lse = high + jnp.log(total)
-            before = top[rows]
+            before = top[:, rows]
             now = jnp.maximum(before, lse)
             keep = jnp.exp(before - now)
             add = jnp.exp(lse - now)
-            num[rows] = num[rows] * keep + part * add
-            den[rows] = den[rows] * keep + add
-            top[rows] = now
+            num[:, rows] = num[:, rows] * keep + part * add
+            den[:, rows] = den[:, rows] * keep + add
+            top[:, rows] = now
 
     def fresh_step(live):
         first = scalars[n] * tok_rows
-        seen = lax.broadcasted_iota(jnp.int32, (tok_rows, live), 1) <= (
-            first + lax.broadcasted_iota(jnp.int32, (tok_rows, live), 0)
+        seen = lax.broadcasted_iota(jnp.int32, (live, tok_rows), 0) <= (
+            first + lax.broadcasted_iota(jnp.int32, (live, tok_rows), 1)
         )
         bias = jnp.where(seen, 0.0, masked_score).astype(jnp.float32)
         for i in range(group):
             rows = slice(i * tok_rows, (i + 1) * tok_rows)
             mixed, high, total = weigh(q_ref[i], fk_ref[:live], fv_ref[:live], bias)
-            before = top[rows]
+            before = top[:, rows]
             now = jnp.maximum(before, high)
             keep = jnp.exp(before - now)
             add = jnp.exp(high - now)
-            value = (num[rows] * keep + mixed * add) / (den[rows] * keep + total * add)
-            out_ref[:, i * HEAD_DIM : (i + 1) * HEAD_DIM] = value.astype(jnp.bfloat16)
+            value = (num[:, rows] * keep + mixed * add) / (den[:, rows] * keep + total * add)
+            out_ref[:, i * HEAD_DIM : (i + 1) * HEAD_DIM] = value.T.astype(jnp.bfloat16)
 
     step = cache_rows // pieces
     fresh_step_rows = fresh_rows // pieces
@@ -394,9 +401,9 @@
             ],
             out_specs=pl.BlockSpec((tok_rows, group * HEAD_DIM), lambda g, c, s: (0, g)),
             scratch_shapes=[
-                pltpu.VMEM((rows, HEAD_DIM), jnp.float32),
-                pltpu.VMEM((rows, 1), jnp.float32),
-                pltpu.VMEM((rows, 1), jnp.float32),
+                pltpu.VMEM((HEAD_DIM, rows), jnp.float32),
+                pltpu.VMEM((1, rows), jnp.float32),
+                pltpu.VMEM((1, rows), jnp.float32),
             ],
         ),
         compiler_params=pltpu.CompilerParams(vmem_limit_bytes=48 * 2**20),

time: 108 us -> 94.4 us (0.87); the launches traced: 109 us -> 93.9 us
  Pallas kernels: 101 us -> 86.1 us
    pallas_call x1, Pallas kernels: 43.8 us -> 28.6 us  [body(): pl.pallas_call(functools.partial(attend_kernel, n), out_shape=jax.ShapeDt...]
where the time goes in v1:
time: 94.4 us; the launch traced here: 93.9 us
  Pallas kernels  86.1 us (91%)
  local copies, waits for them, and re-layouts  5.3 us (6%)
  other arithmetic  1.82 us (2%)
    pallas_call x1, Pallas kernels, body(): pl.pallas_call(functools.partial(project_kernel, n, heads), out_shape=[ja...  57.5 us
    pallas_call x1, Pallas kernels, body(): pl.pallas_call(functools.partial(attend_kernel, n), out_shape=jax.ShapeDt...  28.6 us
    unnamed x8, local copies, waits for them, and re-layouts  5.3 us

profile of v1, /device:TPU:7, one launch (start us, length us, event | category | flops | bytes accessed | tf_op | source)
XLA Modules:
  0.0 93.9 jit_solution(12415982511316145509)
XLA Ops:
  0.7 0.7 pad_add_fusion.scalars
  1.4 0.3 fusion
  1.7 0.8 pad_maximum_fusion
  2.5 57.5 %gather_project.1 = (bf16[16,128,128]{2,1,0:T(8,128)(2,1)}, bf16[8,1024,256]{2,1,0:T(8,128)(2,1)}, bf16[8,1024,256]{2,1,0:T(8,128)(2,1)}, bf16[8,128,256]{2,1,0:T(8,128)(2,1)}, bf16[8,128,256]{2,1,0:T(8,128)(2,1)}) custom-call(bf16[128,2048]{1,0:T(8,128)(2,1)} %tok_hbm.1, f32[1,8192]{1,0:T(1,128)} %bitcast.8, bf16[8192,2048]{1,0:T(8,128)(2,1)} %wq_hbm.1, ...), custom_call_target="tpu_custom_call" | custom-call | tf_op jit(solution)/shard_map/gather_project/pallas_call | solution.py:344
  60.0 0.0 copy-start
  60.0 2.2 %copy-done = bf16[8,1024,256]{2,1,0:T(8,128)(2,1)S(1)} copy-done((bf16[8,1024,256]{2,1,0:T(8,128)(2,1)S(1)}, bf16[8,1024,256]{2,1,0:T(8,128)(2,1)}, u32[]{:S(2)}) %copy-start) | copy-done | bytes 4194328
  62.2 0.0 copy-start.1
  62.2 1.0 %copy-done.1 = bf16[16,128,128]{2,1,0:T(8,128)(2,1)S(1)} copy-done((bf16[16,128,128]{2,1,0:T(8,128)(2,1)S(1)}, bf16[16,128,128]{2,1,0:T(8,128)(2,1)}, u32[]{:S(2)}) %copy-start.1) | copy-done | bytes 524312
  63.2 0.0 copy-start.2
  63.2 1.0 %copy-done.2 = bf16[8,128,256]{2,1,0:T(8,128)(2,1)S(1)} copy-done((bf16[8,128,256]{2,1,0:T(8,128)(2,1)S(1)}, bf16[8,128,256]{2,1,0:T(8,128)(2,1)}, u32[]{:S(2)}) %copy-start.2) | copy-done | bytes 524312
  64.3 0.0 copy-start.3
  64.3 1.0 %copy-done.3 = bf16[8,128,256]{2,1,0:T(8,128)(2,1)S(1)} copy-done((bf16[8,128,256]{2,1,0:T(8,128)(2,1)S(1)}, bf16[8,128,256]{2,1,0:T(8,128)(2,1)}, u32[]{:S(2)}) %copy-start.3) | copy-done | bytes 524312
  65.3 28.6 %attend.1 = bf16[128,2048]{1,0:T(8,128)(2,1)} custom-call(s32[9]{0:T(128)S(1)} %pad_add_fusion.scalars, bf16[16,128,128]{2,1,0:T(8,128)(2,1)S(1)} %copy-done.1, bf16[8,1024,256]{2,1,0:T(8,128)(2,1)S(1)} %copy-done, bf16[8,1024,256]{2,1,0:T(8,128)(2,1)} %get-tuple-element.12.v_ref, bf16[1024,256]{1,0:T(8,128)(2,1)S(1)} %bitcast.6, bf16[1024,256]{1,0:T(8,128)(2,1)S(1)} %bitcast.7), custom_call_target="tpu_custom_call" | custom-call | tf_op jit(solution)/shard_map/attend/pallas_call | solution.py:389
  (2 shorter events, 0.0 us)
Async XLA Ops:
  60.0 2.2 %copy-start = (bf16[8,1024,256]{2,1,0:T(8,128)(2,1)S(1)}, bf16[8,1024,256]{2,1,0:T(8,128)(2,1)}, u32[]{:S(2)}) copy-start(bf16[8,1024,256]{2,1,0:T(8,128)(2,1)} %get-tuple-element.11.k_ref) | copy-start | bytes 12582916
  62.2 1.0 %copy-start.1 = (bf16[16,128,128]{2,1,0:T(8,128)(2,1)S(1)}, bf16[16,128,128]{2,1,0:T(8,128)(2,1)}, u32[]{:S(2)}) copy-start(bf16[16,128,128]{2,1,0:T(8,128)(2,1)} %get-tuple-element.10.q_ref) | copy-start | bytes 1572868
  63.2 1.0 %copy-start.2 = (bf16[8,128,256]{2,1,0:T(8,128)(2,1)S(1)}, bf16[8,128,256]{2,1,0:T(8,128)(2,1)}, u32[]{:S(2)}) copy-start(bf16[8,128,256]{2,1,0:T(8,128)(2,1)} %get-tuple-element.13) | copy-start | bytes 1572868
  64.3 1.0 %copy-start.3 = (bf16[8,128,256]{2,1,0:T(8,128)(2,1)S(1)}, bf16[8,128,256]{2,1,0:T(8,128)(2,1)}, u32[]{:S(2)}) copy-start(bf16[8,128,256]{2,1,0:T(8,128)(2,1)} %get-tuple-element.14) | copy-start | bytes 1572868
